TPU v7x, 128 devices: a whole 4x4x4 slice. The times are simulated.
128 devices in a mesh: fsdp: 8 (over y, core), seq: 16 (over z, x).
Axes of the slice: x: 4, y: 4, z: 4, core: 2. Of those that a mesh axis runs over, the one named last changes fastest.
Arguments:
- queries: bfloat16 [8, 8192, 2048], P('fsdp', 'seq'), may hold values from -6 to 6
- keys: bfloat16 [8, 8192, 2048], P('fsdp', 'seq'), may hold values from -6 to 6
- values: bfloat16 [8, 8192, 2048], P('fsdp', 'seq'), may hold values from -6 to 6
- gates: bfloat16 [8, 8192, 2048], P('fsdp', 'seq'), may hold values from -6 to 6
- log_decay: float32 [8, 16, 8192], P('fsdp', None, 'seq'), may hold values from -1 to 0, as said below
- out_weight: bfloat16 [2048, 2048], P('fsdp'), may hold values from -0.125 to 0.125
- grad_out: bfloat16 [8, 8192, 2048], P('fsdp', 'seq'), may hold values from -6 to 6
Outputs:
- output: bfloat16 [8, 8192, 2048], P('fsdp', 'seq')
- grad_queries: bfloat16 [8, 8192, 2048], P('fsdp', 'seq')
- grad_keys: bfloat16 [8, 8192, 2048], P('fsdp', 'seq')
- grad_values: bfloat16 [8, 8192, 2048], P('fsdp', 'seq')
- grad_gates: bfloat16 [8, 8192, 2048], P('fsdp', 'seq')
- grad_weight: float32 [2048, 2048], P(('fsdp', 'seq'))
Inputs may be any that keep to these rules, and one draw needn't show every extreme that they name: `log_decay`: every value is negative.
All inputs are finite; a program needn't handle non-finite values.
Results may differ from a plain program's by a relative error of at most 0.018.
Values may be sent and summed in bfloat16 or wider, within the bound.
No kernel may reach another device: no remote copies, remote signals or barrier semaphores. Data moves between devices by JAX's collectives and lax.ppermute only.
A program may use at most 256 MiB of HBM per device.

v0:
```python
import math

import jax
import jax.numpy as jnp
from jax import lax
from jax.sharding import PartitionSpec as P

TRIPLE = lax.Precision.HIGH


def carried_in(x, axis, combine, identity):
    peers, index = (lax.axis_size(axis), lax.axis_index(axis))
    everything = jax.tree.map(
        lambda part, kind: lax.all_gather(part.astype(kind), axis), x, (jnp.bfloat16, jnp.bfloat16)
    )
    start = jax.tree.map(
        lambda part, zero: jnp.broadcast_to(jnp.asarray(zero, part.dtype), part.shape), x, identity
    )

    def carried_turn(k, before):
        reached = k < index
        new = combine(
            before, jax.tree.map(lambda part, own: part[k].astype(own.dtype), everything, x)
        )
        return jax.tree.map(lambda a, b: jnp.where(reached, a, b), new, before)

    return lax.fori_loop(0, peers, carried_turn, start)


def entering(x, axis, combine, identity):
    peers, index = (lax.axis_size(axis), lax.axis_index(axis))
    everything = jax.tree.map(
        lambda part, kind: lax.all_gather(part.astype(kind), axis),
        x,
        jax.tree.map(lambda a: jnp.bfloat16 if a.dtype == jnp.float32 else a.dtype, x),
    )
    start = jax.tree.map(
        lambda part, zero: jnp.broadcast_to(jnp.asarray(zero, part.dtype), part.shape), x, identity
    )

    def entering_turn(k, before):
        at = peers - 1 - k
        reached = at > index
        new = combine(
            before, jax.tree.map(lambda part, own: part[at].astype(own.dtype), everything, x)
        )
        return jax.tree.map(lambda a, b: jnp.where(reached, a, b), new, before)

    return lax.fori_loop(0, peers, entering_turn, start)


def local_output(query_f, key_f, value_f, cumul, state):
    length = query_f.shape[0]
    scores = jnp.einsum("thd,shd->hts", query_f, key_f, precision=TRIPLE)
    gap = cumul[:, :, None] - cumul[:, None, :]
    causal = lax.broadcasted_iota(jnp.int32, (length, length), 0) >= lax.broadcasted_iota(
        jnp.int32, (length, length), 1
    )
    weights = jnp.where(causal, jnp.exp(jnp.where(causal, gap, 0.0)), 0.0)
    inner = jnp.einsum("hts,she->the", weights * scores, value_f, precision=TRIPLE)
    carried = (
        jnp.einsum("thd,hde->the", query_f, state, precision=TRIPLE) * jnp.exp(cumul).T[:, :, None]
    )
    return inner + carried


def normalize(mixed, gate_f):
    length = mixed.shape[0]
    scaled = mixed * lax.rsqrt(jnp.mean(mixed * mixed, axis=-1, keepdims=True) + 1e-05)
    return scaled.reshape(length, -1) * jax.nn.silu(gate_f)


def combine_states(earlier, later):
    return (earlier[0] + later[0], jnp.exp(later[0])[:, None, None] * earlier[1] + later[1])


def shards(queries, keys, values, gates, log_decay, out_weight, grad_out):
    length = queries.shape[1]
    width = queries.shape[2]
    heads = log_decay.shape[1]
    head_dim = width // heads
    query_f = queries[0].astype(jnp.float32).reshape(length, heads, head_dim)
    key_f = keys[0].astype(jnp.float32).reshape(length, heads, head_dim)
    value_f = values[0].astype(jnp.float32).reshape(length, heads, head_dim)
    gate_f = gates[0].astype(jnp.float32)
    cotangent = grad_out[0]
    cumul = jnp.cumsum(log_decay[0], axis=1)
    ending = cumul[:, -1]
    tail = jnp.exp(ending[:, None] - cumul)
    own_state = jnp.einsum("shd,hs,she->hde", key_f, tail, value_f, precision=TRIPLE)
    blank = (jnp.zeros((heads,), jnp.float32), jnp.zeros((heads, head_dim, head_dim), jnp.float32))
    incoming = carried_in((ending, own_state), "seq", combine_states, blank)[1]

    def attend(q_in, k_in, v_in):
        return local_output(q_in, k_in, v_in, cumul, incoming)

    mixed, pull_mix = jax.vjp(attend, query_f, key_f, value_f)
    hidden_f, pull_finish = jax.vjp(normalize, mixed, gate_f)
    hidden = hidden_f.astype(jnp.bfloat16)
    whole = lax.all_gather(out_weight, "fsdp", axis=0, tiled=True)
    result = jnp.dot(hidden, whole, preferred_element_type=jnp.float32)
    grad_hidden = lax.dot_general(
        cotangent, whole, (((1,), (1,)), ((), ())), preferred_element_type=jnp.float32
    )
    grad_mixed, grad_gate = pull_finish(grad_hidden)
    grad_q, grad_k, grad_v = pull_mix(grad_mixed)
    later_term = jnp.einsum(
        "thd,ht,the->hde", query_f, jnp.exp(cumul), grad_mixed, precision=TRIPLE
    )
    returning = entering((ending, later_term), "seq", combine_states, blank)[1]
    tail_rows = tail.T[:, :, None]
    grad_k = grad_k + jnp.einsum("hde,she->shd", returning, value_f, precision=TRIPLE) * tail_rows
    grad_v = grad_v + jnp.einsum("hde,shd->she", returning, key_f, precision=TRIPLE) * tail_rows
    scale = 1.0 / math.sqrt(length * lax.axis_size("seq") * lax.axis_size("fsdp"))
    summed = lax.psum_scatter(
        lax.dot_general(
            hidden, cotangent, (((0,), (0,)), ((), ())), preferred_element_type=jnp.float32
        ),
        ("fsdp", "seq"),
        scatter_dimension=0,
        tiled=True,
    )
    grad_weight = summed * scale
    return (
        result.astype(jnp.bfloat16)[None],
        grad_q.reshape(length, width).astype(jnp.bfloat16)[None],
        grad_k.reshape(length, width).astype(jnp.bfloat16)[None],
        grad_v.reshape(length, width).astype(jnp.bfloat16)[None],
        grad_gate.astype(jnp.bfloat16)[None],
        grad_weight,
    )


def solution(mesh):
    return jax.shard_map(
        shards,
        mesh=mesh,
        in_specs=(
            P("fsdp", "seq", None),
            P("fsdp", "seq", None),
            P("fsdp", "seq", None),
            P("fsdp", "seq", None),
            P("fsdp", None, "seq"),
            P("fsdp", None),
            P("fsdp", "seq", None),
        ),
        out_specs=(
            P("fsdp", "seq", None),
            P("fsdp", "seq", None),
            P("fsdp", "seq", None),
            P("fsdp", "seq", None),
            P("fsdp", "seq", None),
            P(("fsdp", "seq"), None),
        ),
        check_vma=False,
    )
```

profile of v0, /device:TPU:0, one launch (start us, length us, event | category | flops | bytes accessed | tf_op | source)
XLA Modules:
  0.0 934.1 jit_solution(9986887296943799474)
XLA Ops:
  10.1 3.9 copy.95
  14.0 2.3 copy.123
  17.7 2.0 fusion.81
  22.6 42.3 %all-reduce = bf16[256]{0:T(256)(128)(2,1)S(1)} all-reduce(bf16[256]{0:T(256)(128)(2,1)S(1)} %dynamic-update-slice), channel_id=2, replica_groups=mesh['fsdp'=8,'seq'=16] {'seq'}, use_global_device_ids=true, to_apply=%add | all-reduce | flops 256 | bytes 1024
  65.0 3.5 copy.122
  68.5 4.2 copy.112
  72.8 10.8 %fusion.64 = f32[16,512,512]{2,1,0:T(8,128)} fusion(bf16[512,16,128]{2,1,0:T(8,128)(2,1)} %bitcast.136, bf16[512,16,128]{2,1,0:T(8,128)(2,1)} %bitcast.131), kind=kOutput, calls=%fused_computation.78 | convolution fusion | flops 1073741824 | bytes 20971520 | tf_op jit(solution)/shard_map/jvp(thd,shd->hts)/dot_general | solution.py:54
  83.5 14.0 %fusion.6 = f32[16,512,128]{1,2,0:T(8,128)} fusion(bf16[512,16,128]{0,2,1:T(8,128)(2,1)S(1)} %bitcast.141, f32[16,512,512]{2,1,0:T(8,128)} %fusion.64, f32[16,512]{1,0:T(8,128)S(1)} %copy_bitcast_fusion, pred[512,512]{1,0:T(8,128)(4,1)S(1)} %iota_compare_fusion), kind=kOutput, calls=%fused_computation.10 | convolution fusion | flops 3238002688 | bytes 23363584 | tf_op jit(solution)/shard_map/jvp(hts,she->the)/dot_general | solution.py:60
  97.6 11.5 %fusion.61 = (f32[512,2048]{1,0:T(8,128)}, f32[512,2048]{1,0:T(8,128)}) fusion(bf16[1,512,2048]{2,1,0:T(8,128)(2,1)} %param.14, bf16[2048,2048]{1,0:T(8,128)(2,1)} %all-gather.7.cloned.1.call-done, bf16[1,512,2048]{2,1,0:T(8,128)(2,1)S(1)} %copy-done), kind=kOutput, calls=%fused_computation.75 | convolution fusion | flops 4301258752 | bytes 20971520 | tf_op jit(solution)/shard_map/dot_general | solution.py:102
  109.1 5.4 copy.101
  114.5 21.3 %all-gather.9.cloned.1.call-done = bf16[256,128,128]{2,1,0:T(8,128)(2,1)} async-done(((bf16[16,128,128]{2,1,0:T(8,128)(2,1)}), bf16[256,128,128]{2,1,0:T(8,128)(2,1)}) %all-gather.9.cloned.1.call-update) | async-done | bytes 8388624 | tf_op jit(solution)/shard_map/all_gather | solution.py:14
  135.7 21.5 %while.30 = (s32[]{:T(128)}, f32[16,128,128]{2,1,0:T(8,128)S(1)}, s32[]{:T(128)}, bf16[16,16]{1,0:T(8,128)(2,1)S(1)}, bf16[16,16,128,128]{3,2,1,0:T(8,128)(2,1)}, /*index=5*/s32[]{:T(128)}, s32[]{:T(128)}) while((s32[]{:T(128)}, f32[16,128,128]{2,1,0:T(8,128)S(1)}, s32[]{:T(128)}, bf16[16,16]{1,0:T(8,128)(2,1)S(1)}, ...), condition=%wide.region_3.4_spmd.clone, body=%wide.region_2.3_spmd.clone.sunk | while | flops 1310740 | bytes 2621705 | solution.py:27
  157.3 7.3 multiply_reduce_fusion
  164.6 3.7 multiply_convert_fusion
  168.3 2.0 copy-done.2
  170.3 2.0 fusion.86
  173.4 9.9 %fusion.51 = f32[2048,2048]{1,0:T(8,128)} fusion(bf16[512,2048]{0,1:T(8,128)(2,1)} %bitcast.150, bf16[1,512,2048]{2,1,0:T(8,128)(2,1)S(1)} %copy-done), kind=kOutput, calls=%fused_computation.66 | convolution fusion | flops 4294967296 | bytes 20971520 | tf_op jit(solution)/shard_map/dot_general | solution.py:116
  184.6 4.3 fusion.38
  188.9 8.4 fusion.36
  197.3 14.0 %add_convert_fusion = bf16[16,512,128]{1,2,0:T(8,128)(2,1)} fusion(f32[16,512,128]{1,2,0:T(8,128)S(1)} %fusion.38, f32[16,512,512]{2,1,0:T(8,128)} %fusion.36, f32[16,512]{1,0:T(8,128)S(1)} %copy_bitcast_fusion, pred[512,512]{1,0:T(8,128)(4,1)S(1)} %iota_compare_fusion, bf16[512,16,128]{2,1,0:T(8,128)(2,1)S(1)} %bitcast.137), kind=kOutput, calls=%fused_computation.54 | convolution fusion | flops 3240099840 | bytes 25460736 | tf_op jit(solution)/shard_map/transpose(jvp(thd,shd->hts))/dot_general | solution.py:54
  211.3 3.9 copy.113
  215.2 5.6 copy.100
  220.8 5.8 fusion.58
  226.7 14.1 %fusion.4 = f32[16,128,512]{2,1,0:T(8,128)} fusion(f32[16,512,512]{2,1,0:T(8,128)} %fusion.64, f32[16,512]{1,0:T(8,128)S(1)} %copy_bitcast_fusion, pred[512,512]{1,0:T(8,128)(4,1)S(1)} %iota_compare_fusion, f32[512,16,128]{0,2,1:T(8,128)S(1)} %copy-done.4), kind=kOutput, calls=%fused_computation.9 | convolution fusion | flops 3238002688 | bytes 25460736 | tf_op jit(solution)/shard_map/transpose(jvp(hts,she->the))/dot_general | solution.py:60
  240.8 13.7 %fusion.8 = f32[16,512,128]{1,2,0:T(8,128)} fusion(f32[16,512,512]{2,1,0:T(8,128)} %fusion.36, f32[16,512]{1,0:T(8,128)S(1)} %copy_bitcast_fusion, pred[512,512]{1,0:T(8,128)(4,1)S(1)} %iota_compare_fusion, bf16[512,16,128]{2,1,0:T(8,128)(2,1)S(1)} %bitcast.134), kind=kOutput, calls=%fused_computation.11 | convolution fusion | flops 3238002688 | bytes 23363584 | tf_op jit(solution)/shard_map/transpose(jvp(thd,shd->hts))/dot_general | solution.py:54
  254.5 6.2 fusion.50
  260.7 21.7 %while.31 = (s32[]{:T(128)}, f32[16,128,128]{2,1,0:T(8,128)S(1)}, s32[]{:T(128)}, bf16[16,16]{1,0:T(8,128)(2,1)S(1)}, bf16[16,16,128,128]{3,2,1,0:T(8,128)(2,1)}...) while((s32[]{:T(128)}, f32[16,128,128]{2,1,0:T(8,128)S(1)}, s32[]{:T(128)}, ...), condition=%wide.region_7.8_spmd.clone, body=%wide.region_6.7_spmd.clone.sunk | while | flops 1310744 | bytes 2621767 | solution.py:49
  260.8 1.4 fusion.111
  262.3 1.3 fusion.111
  263.6 1.3 fusion.111
  264.9 1.3 fusion.111
  266.3 1.3 fusion.111
  267.6 1.3 fusion.111
  269.0 1.3 fusion.111
  270.3 1.3 fusion.111
  271.7 1.3 fusion.111
  273.0 1.3 fusion.111
  274.4 1.3 fusion.111
  275.7 1.3 fusion.111
  277.1 1.3 fusion.111
  278.4 1.3 fusion.111
  279.8 1.3 fusion.111
  282.4 5.6 fusion.32
  288.1 3.9 copy.115
  292.0 5.7 fusion.34
  297.7 3.9 copy.114
  301.6 623.9 %reduce-scatter.2.cloned.1.call-done = f32[16,2048]{1,0:T(8,128)} async-done(((f32[2048,2048]{1,0:T(8,128)}), f32[16,2048]{1,0:T(8,128)}) %reduce-scatter.2.cloned.1.call-update) | async-done | bytes 131088 | tf_op jit(solution)/shard_map/reduce_scatter | solution.py:115
  925.6 1.6 broadcast_multiply_fusion.1
  (125 shorter events, 31.2 us)
Async XLA Ops:
  7.2 90.4 %copy-start = (bf16[1,512,2048]{2,1,0:T(8,128)(2,1)S(1)}, bf16[1,512,2048]{2,1,0:T(8,128)(2,1)}, u32[]{:S(2)}) copy-start(bf16[1,512,2048]{2,1,0:T(8,128)(2,1)} %param.17) | copy-start | bytes 6291460
  7.2 90.4 %all-gather.7.cloned.1.call-start = ((), (), s32[]{:S(2)}) async-start(), calls=%async_computation.1 | async-start | bytes 9437184 | tf_op jit(solution)/shard_map/all_gather | solution.py:100
  7.9 127.8 %all-gather.9.cloned.1.call-start = ((), (), s32[]{:S(2)}) async-start(), calls=%async_computation.3 | async-start | bytes 8912896 | tf_op jit(solution)/shard_map/all_gather | solution.py:14
  14.0 3.7 copy-start.13
  16.4 1.4 copy-start.10
  16.4 4.5 copy-start.20
  20.8 239.9 %all-gather.11.cloned.1.call-start = ((), (), s32[]{:S(2)}) async-start(), calls=%async_computation.4 | async-start | bytes 8912896 | tf_op jit(solution)/shard_map/all_gather | solution.py:33
  72.7 10.8 %copy-start.14 = (bf16[1,512,2048]{1,2,0:T(8,128)(2,1)S(1)}, bf16[1,512,2048]{1,2,0:T(8,128)(2,1)}, u32[]{:S(2)}) copy-start(bf16[1,512,2048]{1,2,0:T(8,128)(2,1)} %copy.95) | copy-start | bytes 6291460
  157.2 7.3 copy-start.5
  157.2 7.3 copy-start.7
  157.2 7.3 copy-start.17
  164.6 5.7 copy-start.8
  168.3 2.0 copy-start.2
  173.4 752.2 %reduce-scatter.2.cloned.1.call-start = ((), (), s32[]{:S(2)}) async-start(), calls=%async_computation.2 | async-start | bytes 16908288 | tf_op jit(solution)/shard_map/reduce_scatter | solution.py:115
  183.3 1.3 copy-start.6
  184.6 4.3 copy-start.3
  184.6 4.3 copy-start.15
  188.9 8.4 copy-start.11
  215.2 5.6 copy-start.18
  220.8 5.9 copy-start.4
  226.7 14.1 %copy-start.9 = (bf16[64,8,16,128]{3,2,1,0:T(8,128)(2,1)S(1)}, bf16[64,8,16,128]{3,2,1,0:T(8,128)(2,1)}, u32[]{:S(2)}) copy-start(bf16[64,8,16,128]{3,2,1,0:T(8,128)(2,1)} %copy.122) | copy-start | bytes 6291460
  226.7 27.8 %slice-start = ((s8[8388608]{0:T(1024)(128)(4,1)}), s8[4194304]{0:T(1024)(128)(4,1)S(1)}, s32[]{:S(2)}) async-start(s8[8388608]{0:T(1024)(128)(4,1)} %bitcast.153), calls=%async_computation.5 | async-start | bytes 8388608
  240.8 13.7 %copy-start.16 = (f32[512,2048]{1,0:T(8,128)S(1)}, f32[512,2048]{1,0:T(8,128)}, u32[]{:S(2)}) copy-start(f32[512,2048]{1,0:T(8,128)} %copy.100) | copy-start | bytes 12582916
  240.8 13.7 %copy-start.19 = (bf16[1,512,2048]{2,1,0:T(8,128)(2,1)S(1)}, bf16[1,512,2048]{2,1,0:T(8,128)(2,1)}, u32[]{:S(2)}) copy-start(bf16[1,512,2048]{2,1,0:T(8,128)(2,1)} %param.14) | copy-start | bytes 6291460
  240.8 13.7 %slice-start.1 = ((s8[8388608]{0:T(1024)(128)(4,1)}), s8[4194304]{0:T(1024)(128)(4,1)S(1)}, s32[]{:S(2)}) async-start(s8[8388608]{0:T(1024)(128)(4,1)} %bitcast.153), calls=%async_computation.6 | async-start | bytes 8388608
  260.7 21.7 %copy-start.12 = (bf16[64,8,16,128]{3,2,1,0:T(8,128)(2,1)S(1)}, bf16[64,8,16,128]{3,2,1,0:T(8,128)(2,1)}, u32[]{:S(2)}) copy-start(bf16[64,8,16,128]{3,2,1,0:T(8,128)(2,1)} %copy-done.10) | copy-start | bytes 6291460
  292.0 635.2 %copy-start.1 = (bf16[1,512,2048]{2,1,0:T(8,128)(2,1)S(1)}, bf16[1,512,2048]{2,1,0:T(8,128)(2,1)}, u32[]{:S(2)}) copy-start(bf16[1,512,2048]{2,1,0:T(8,128)(2,1)} %param.17) | copy-start | bytes 6291460
Sparse Core Ops, SparseCore 0:
  9.7 52.1 all-gather.6
  64.7 71.0 all-gather.8
  173.5 70.4 all-gather.10
  246.2 679.3 reduce-scatter.1
where the time goes:
time: 940 us; the launch traced here: 934 us
  waiting for transfers between devices  646 us (69%)
  matrix products  130 us (14%)
  other arithmetic  54.5 us (6%)
  local copies, waits for them, and re-layouts  45.3 us (5%)
  blocking collectives  42.3 us (4%)
  between operations  15.1 us (2%)
    reduce_scatter x1, waiting for transfers between devices, shards(): lax.psum_scatter(lax.dot_general(hidden, cotangent, (((0,), (0,)), ((), (...  624 us
    unnamed x1, blocking collectives  42.3 us
    dot_general x3, matrix products, local_output(): scores = jnp.einsum('thd,shd->hts', query_f, key_f, precision=TRIPLE)  38.4 us
    dot_general x3, matrix products, local_output(): jnp.einsum('hts,she->the', weights * scores, value_f, precision=TRIPLE)  36.5 us
    unnamed x55, local copies, waits for them, and re-layouts  26.6 us
    all_gather x1, waiting for transfers between devices, carried_in(): lax.all_gather(part.astype(kind), axis)  21.3 us
    select_n x16, other arithmetic, entering_turn(): return jax.tree.map(lambda a, b: jnp.where(reached, a, b), new, before)  20.9 us
    select_n x16, other arithmetic, carried_turn(): return jax.tree.map(lambda a, b: jnp.where(reached, a, b), new, before)  20.6 us
  transfers between devices with their start and end apart: 4, of which 2 were waited for; matrix products, arithmetic and copies ran while one was open for 20% of the time, Pallas kernels for 0%

commit v1 on v0

v1 whole, which is shorter than its diff:
```python
import functools
import math

import jax
import jax.numpy as jnp
from jax import lax
from jax.experimental import pallas as pl
from jax.experimental.pallas import tpu as pltpu
from jax.sharding import Mesh
from jax.sharding import PartitionSpec as P

F32 = jnp.float32
BF16 = jnp.bfloat16
HIGHEST = lax.Precision.HIGHEST
CHUNK = 256
HEAD = 128
VMEM = 56
GROUP = 4
TOP = 16
EXTRA = 16
NN = (((1,), (0,)), ((), ()))
NT = (((1,), (1,)), ((), ()))
TN = (((0,), (0,)), ((), ()))
FSDP = ("y", "core")
SEQ = ("z", "x")


def dot(a, b, dims, precision=None):
    return lax.dot_general(a, b, dims, precision=precision, preferred_element_type=F32)


def causal(shape):
    return lax.broadcasted_iota(jnp.int32, shape, 0) >= lax.broadcasted_iota(jnp.int32, shape, 1)


def params(mib=VMEM):
    return pltpu.CompilerParams(
        dimension_semantics=("arbitrary",), vmem_limit_bytes=mib * 1024 * 1024
    )


def three_parts(x):
    hi = x.astype(BF16)
    mid = (x - hi.astype(F32)).astype(BF16)
    lo = (x - hi.astype(F32) - mid.astype(F32)).astype(BF16)
    return hi, mid, lo


def states_kernel(ld_ref, k_ref, v_ref, row_ref, col_ref, first_ref, own_ref):
    chunks = ld_ref.shape[2] // CHUNK
    lower = jnp.where(causal((CHUNK, CHUNK)), 1.0, 0.0).astype(F32)
    for c in range(chunks):
        t = slice(c * CHUNK, (c + 1) * CHUNK)
        part = ld_ref[0, :, t]
        row_ref[0, :, t] = dot(part, lower, NT, HIGHEST)
        col_ref[0, t, :] = dot(lower, part, NT, HIGHEST)
    for h in range(GROUP):
        w = slice(h * HEAD, (h + 1) * HEAD)
        state, total = None, None
        for c in range(chunks):
            t = slice(c * CHUNK, (c + 1) * CHUNK)
            a = col_ref[0, t, h : h + 1]
            end = a[CHUNK - 1 : CHUNK]
            scaled = (v_ref[t, w].astype(F32) * jnp.exp(end - a)).astype(BF16)
            new = dot(k_ref[t, w], scaled, TN)
            if c == 0:
                state, total = new, end
                first_ref[h] = new.astype(BF16)
            else:
                state, total = state * jnp.exp(end) + new, total + end
        own_ref[h, :HEAD, :] = state.astype(BF16)
        hi, mid, lo = (p.astype(F32) for p in three_parts(total))
        at = lax.broadcasted_iota(jnp.int32, (EXTRA, HEAD), 0)
        rows = jnp.where(at == 0, hi, jnp.where(at == 1, mid, jnp.where(at == 2, lo, 0.0)))
        own_ref[h, HEAD:, :] = rows.astype(BF16)


def scan_kernel(reverse, parts_ref, decay_ref, ordered_ref, out_ref):
    peers = out_ref.shape[0]
    state = jnp.zeros(out_ref.shape[1:], F32)
    for j in reversed(range(peers)) if reverse else range(peers):
        out_ref[j] = state.astype(BF16)
        rows = decay_ref[j, HEAD:, :].astype(F32)
        decay = jnp.exp(rows[0:1] + rows[1:2] + rows[2:3])
        state = state * decay + parts_ref[j, :HEAD, :].astype(F32)


def decays(row_ref, col_ref, h, c):
    t = slice(c * CHUNK, (c + 1) * CHUNK)
    a = col_ref[0, t, h : h + 1]
    row = row_ref[0, h : h + 1, t]
    weights = jnp.exp(jnp.where(causal((CHUNK, CHUNK)), a - row, -1e30))
    return a, weights


def sigmoid(x):
    return 0.5 + 0.5 * jnp.tanh(0.5 * x)


def inner_kernel(q_ref, k_ref, v_ref, row_ref, col_ref, inner_ref, top_ref):
    chunks = q_ref.shape[0] // CHUNK
    for h in range(GROUP):
        w = slice(h * HEAD, (h + 1) * HEAD)
        for c in range(chunks):
            t = slice(c * CHUNK, (c + 1) * CHUNK)
            _, weights = decays(row_ref, col_ref, h, c)
            scores = (dot(q_ref[t, w], k_ref[t, w], NT) * weights).astype(BF16)
            inner = dot(scores, v_ref[t, w], NN)
            inner_ref[t, w] = inner.astype(BF16)
            if c == 0:
                top_ref[:, w] = inner[:TOP]


def carry_kernel(
    inner_ref, top_ref, q_ref, g_ref, col_ref, in_ref, first_ref,
    norm_ref, norm_top_ref, rms_ref, hidden_ref,
):
    chunks = q_ref.shape[0] // CHUNK
    for h in range(GROUP):
        w = slice(h * HEAD, (h + 1) * HEAD)
        state = in_ref[h]
        for c in range(chunks):
            t = slice(c * CHUNK, (c + 1) * CHUNK)
            a = col_ref[0, t, h : h + 1]
            inner = inner_ref[t, w].astype(F32)
            if c == 0:
                inner = jnp.concatenate([top_ref[:, w], inner[TOP:]], axis=0)
            mixed = inner + dot(q_ref[t, w], state, NN) * jnp.exp(a)
            if c + 1 < chunks:
                end = jnp.exp(a[CHUNK - 1 : CHUNK])
                state = (state.astype(F32) * end + first_ref[h].astype(F32)).astype(BF16)
            rms = lax.rsqrt(jnp.mean(mixed * mixed, axis=-1, keepdims=True) + 1e-05)
            normal = mixed * rms
            gate = g_ref[t, w].astype(F32)
            norm_ref[t, w] = normal.astype(BF16)
            if c == 0:
                norm_top_ref[:, w] = normal[:TOP]
            rms_ref[0, t, h : h + 1] = rms
            hidden_ref[t, w] = (normal * (gate * sigmoid(gate))).astype(BF16)


def middle_kernel(
    cot_ref, weight_ref, norm_ref, norm_top_ref, rms_ref, g_ref, q_ref, col_ref,
    gate_ref, dm_ref, dm_low_ref, last_ref, own_ref,
):
    chunks = q_ref.shape[0] // CHUNK
    grad_hidden = dot(cot_ref[...], weight_ref[...], NT)
    for h in range(GROUP):
        w = slice(h * HEAD, (h + 1) * HEAD)
        state = None
        for c in reversed(range(chunks)):
            t = slice(c * CHUNK, (c + 1) * CHUNK)
            gh = grad_hidden[t, w]
            normal = norm_ref[t, w].astype(F32)
            if c == 0:
                normal = jnp.concatenate([norm_top_ref[:, w], normal[TOP:]], axis=0)
            gate = g_ref[t, w].astype(F32)
            open_part = sigmoid(gate)
            silu = gate * open_part
            slope = open_part + silu - silu * open_part
            gate_ref[t, w] = (gh * normal * slope).astype(BF16)
            dn = gh * silu
            dm = rms_ref[0, t, h : h + 1] * (
                dn - normal * jnp.mean(dn * normal, axis=-1, keepdims=True)
            )
            high = dm.astype(BF16)
            dm_ref[t, w] = high
            if c == 0:
                dm_low_ref[:, w] = (dm[:TOP] - high[:TOP].astype(F32)).astype(BF16)
            a = col_ref[0, t, h : h + 1]
            new = dot(q_ref[t, w], (dm * jnp.exp(a)).astype(BF16), TN)
            if state is None:
                state = new
                last_ref[h] = new.astype(BF16)
            else:
                state = state * jnp.exp(a[CHUNK - 1 : CHUNK]) + new
        own_ref[h] = state.astype(BF16)


def backward_kernel(
    q_ref, k_ref, v_ref, dm_ref, dm_low_ref, row_ref, col_ref, in_ref, first_ref, ordered_ref,
    dq_ref, dk_ref, dv_ref,
):
    chunks = q_ref.shape[0] // CHUNK
    for h in range(GROUP):
        w = slice(h * HEAD, (h + 1) * HEAD)
        state = in_ref[h]
        for c in range(chunks):
            t = slice(c * CHUNK, (c + 1) * CHUNK)
            a, weights = decays(row_ref, col_ref, h, c)
            q, k, v, dm = q_ref[t, w], k_ref[t, w], v_ref[t, w], dm_ref[t, w]
            scores = (dot(q, k, NT) * weights).astype(BF16)
            ds = dot(dm, v, NT)
            if c == 0:
                ds = jnp.concatenate([ds[:TOP] + dot(dm_low_ref[:, w], v, NT), ds[TOP:]], axis=0)
            ds = (ds * weights).astype(BF16)
            dq = dot(ds, k, NN) + dot(dm, state, NT) * jnp.exp(a)
            dq_ref[t, w] = dq.astype(BF16)
            dk_ref[t, w] = dot(ds, q, TN).astype(BF16)
            dv_ref[t, w] = dot(scores, dm, TN).astype(BF16)
            if c + 1 < chunks:
                end = jnp.exp(a[CHUNK - 1 : CHUNK])
                state = (state.astype(F32) * end + first_ref[h].astype(F32)).astype(BF16)


def output_kernel(hidden_ref, weight_ref, ordered_ref, out_ref):
    out_ref[...] = dot(hidden_ref[...], weight_ref[...], NN).astype(BF16)


def finish_kernel(k_ref, v_ref, pk_ref, pv_ref, col_ref, ret_ref, last_ref, dk_ref, dv_ref):
    chunks = k_ref.shape[0] // CHUNK
    for h in range(GROUP):
        w = slice(h * HEAD, (h + 1) * HEAD)
        state = ret_ref[h]
        for c in reversed(range(chunks)):
            t = slice(c * CHUNK, (c + 1) * CHUNK)
            a = col_ref[0, t, h : h + 1]
            end = a[CHUNK - 1 : CHUNK]
            tail = jnp.exp(end - a)
            dk = pk_ref[t, w].astype(F32) + dot(v_ref[t, w], state, NT) * tail
            dv = pv_ref[t, w].astype(F32) + dot(k_ref[t, w], state, NN) * tail
            dk_ref[t, w] = dk.astype(BF16)
            dv_ref[t, w] = dv.astype(BF16)
            if c > 0:
                state = (state.astype(F32) * jnp.exp(end) + last_ref[h].astype(F32)).astype(BF16)


def shards(queries, keys, values, gates, log_decay, out_weight, grad_out):
    length, width = queries.shape[1:]
    heads = log_decay.shape[1]
    groups = heads // GROUP
    q, k, v, g, cot = (a[0] for a in (queries, keys, values, gates, grad_out))
    ld = log_decay[0].reshape(groups, GROUP, length)

    wide = pl.BlockSpec((length, GROUP * HEAD), lambda i: (0, i))
    top = pl.BlockSpec((TOP, GROUP * HEAD), lambda i: (0, i))
    row = pl.BlockSpec((1, GROUP, length), lambda i: (i, 0, 0))
    col = pl.BlockSpec((1, length, GROUP), lambda i: (i, 0, 0))
    mat = pl.BlockSpec((GROUP, HEAD, HEAD), lambda i: (i, 0, 0))
    message = pl.BlockSpec((GROUP, HEAD + EXTRA, HEAD), lambda i: (i, 0, 0))
    wide_t = jax.ShapeDtypeStruct((length, width), BF16)
    top_f = jax.ShapeDtypeStruct((TOP, width), F32)
    top_t = jax.ShapeDtypeStruct((TOP, width), BF16)
    row_t = jax.ShapeDtypeStruct((groups, GROUP, length), F32)
    col_t = jax.ShapeDtypeStruct((groups, length, GROUP), F32)
    mat_t = jax.ShapeDtypeStruct((heads, HEAD, HEAD), BF16)
    message_t = jax.ShapeDtypeStruct((heads, HEAD + EXTRA, HEAD), BF16)

    def call(body, ins, outs, shapes, us=5):
        return pl.pallas_call(
            body,
            grid=(groups,),
            in_specs=ins,
            out_specs=outs,
            out_shape=shapes,
            compiler_params=params(),
            cost_estimate=pl.CostEstimate(
                flops=us * 600_000_000, bytes_accessed=us * 2_500_000, transcendentals=0
            ),
        )

    whole = lax.all_gather(out_weight, FSDP, axis=0, tiled=True)
    a_row, a_col, first, own = call(
        states_kernel, [row, wide, wide], [row, col, mat, message], [row_t, col_t, mat_t, message_t]
    )(ld, k, v)

    anywhere = pl.BlockSpec(memory_space=pl.ANY)
    vmem = pl.BlockSpec(memory_space=pltpu.VMEM)

    def scan(parts, decay, ordered, reverse):
        return pl.pallas_call(
            functools.partial(scan_kernel, reverse),
            in_specs=[vmem, vmem, anywhere],
            out_shape=jax.ShapeDtypeStruct((parts.shape[0], HEAD, HEAD), BF16),
            compiler_params=pltpu.CompilerParams(vmem_limit_bytes=VMEM * 1024 * 1024),
        )(parts, decay, ordered)

    mine = lax.all_to_all(own, SEQ, 0, 0, tiled=True)
    inner, inner_top = call(
        inner_kernel, [wide, wide, wide, row, col], [wide, top], [wide_t, top_f], us=9
    )(q, k, v, a_row, a_col)
    incoming = lax.all_to_all(scan(mine, mine, inner, False), SEQ, 0, 0, tiled=True)

    normal, normal_top, rms, hidden = call(
        carry_kernel,
        [wide, top, wide, wide, col, mat, mat],
        [wide, top, col, wide],
        [wide_t, top_f, col_t, wide_t],
    )(inner, inner_top, q, g, a_col, incoming, first)

    partial_grad = dot(hidden, cot, TN).astype(BF16)
    part = lax.psum_scatter(partial_grad, FSDP, scatter_dimension=0, tiled=True)

    grad_gate, dm, dm_low, last, later = call(
        middle_kernel,
        [
            pl.BlockSpec((length, cot.shape[1]), lambda i: (0, 0)),
            pl.BlockSpec((GROUP * HEAD, cot.shape[1]), lambda i: (i, 0)),
            wide,
            top,
            col,
            wide,
            wide,
            col,
        ],
        [wide, wide, top, mat, mat],
        [wide_t, wide_t, top_t, mat_t, mat_t],
        us=12,
    )(cot, whole, normal, normal_top, rms, g, q, a_col)
    theirs = lax.all_to_all(later, SEQ, 0, 0, tiled=True)
    result = call(
        output_kernel,
        [
            pl.BlockSpec((length, width), lambda i: (0, 0)),
            pl.BlockSpec((width, GROUP * HEAD), lambda i: (0, i)),
            anywhere,
        ],
        wide,
        wide_t,
        us=8,
    )(hidden, whole, later)
    turned = scan(theirs, mine, result, True)
    returning = lax.all_to_all(turned, SEQ, 0, 0, tiled=True)
    grad_q, part_k, part_v = call(
        backward_kernel,
        [wide, wide, wide, wide, top, row, col, mat, mat, anywhere],
        [wide, wide, wide],
        [wide_t, wide_t, wide_t],
        us=13,
    )(q, k, v, dm, dm_low, a_row, a_col, incoming, first, turned)
    grad_k, grad_v = call(
        finish_kernel, [wide, wide, wide, wide, col, mat, mat], [wide, wide], [wide_t, wide_t]
    )(k, v, part_k, part_v, a_col, returning, last)

    peers = lax.axis_size(SEQ)
    part, _ = lax.optimization_barrier((part, part_k))
    pieces = lax.all_to_all(part, SEQ, 0, 0, tiled=True)
    pieces = pieces.reshape(peers, -1, pieces.shape[1]).astype(F32)
    scale = 1.0 / math.sqrt(length * peers * lax.axis_size(FSDP))
    grad_weight = jnp.sum(pieces, axis=0) * scale
    return (
        result[None],
        grad_q[None],
        grad_k[None],
        grad_v[None],
        grad_gate[None],
        grad_weight,
    )


def solution(mesh):
    cut = Mesh(mesh.devices.reshape(4, 2, 4, 4), FSDP + SEQ)
    tokens = P(FSDP, SEQ, None)
    return jax.shard_map(
        shards,
        mesh=cut,
        in_specs=(tokens, tokens, tokens, tokens, P(FSDP, None, SEQ), P(FSDP, None), tokens),
        out_specs=(tokens, tokens, tokens, tokens, tokens, P(FSDP + SEQ, None)),
        check_vma=False,
    )
```

time: 940 us -> 155 us (0.16)
  waiting for transfers between devices: 646 us -> 15.9 us
  matrix products: 130 us -> 8.44 us
  Pallas kernels: 0 us -> 72 us
  other arithmetic: 54.5 us -> 0.81 us
  local copies, waits for them, and re-layouts: 45.3 us -> 3 us
  blocking collectives: 42.3 us -> 14.7 us
  starting transfers between devices: 0.16 us -> 24.7 us
    reduce_scatter x1, waiting for transfers between devices: 624 us -> 0.02 us  [shards(): part = lax.psum_scatter(partial_grad, FSDP, scatter_dimension=0, tiled=True)]
    dot_general x15 -> x1, matrix products: 130 us -> 8.44 us  [dot(): lax.dot_general(a, b, dims, precision=precision, preferred_element_type=F32)]
    pallas_call x0 -> x9, Pallas kernels: none -> 72 us  [the longest x1 14.2 us: shards(): call(backward_kernel, [wide, wide, wide, wide, top, row, col, mat, mat, a...]
    unnamed x1 -> x0, blocking collectives: 42.3 us -> none
    select_n x32 -> x0, other arithmetic: 41.5 us -> none  [the longest x16 20.9 us: entering_turn(): return jax.tree.map(lambda a, b: jnp.where(reached, a, b), new, before)]
    unnamed x55 -> x8, local copies, waits for them, and re-layouts: 26.6 us -> 1.61 us
    all_to_all x0 -> x4, starting transfers between devices: none -> 24.7 us  [the longest x1 7.96 us: shards(): mine = lax.all_to_all(own, SEQ, 0, 0, tiled=True)]
    all_gather x3 -> x1, waiting for transfers between devices: 21.3 us -> 0.02 us  [shards(): whole = lax.all_gather(out_weight, FSDP, axis=0, tiled=True)]
  transfers between devices with their start and end apart: 4 -> 6, of which waited for: 2 -> 3; matrix products, arithmetic and copies ran while one was open for 20% -> 6% of each run, Pallas kernels for 0% -> 47%
where the time goes in v1:
time: 155 us; the launch traced here: 154 us
  Pallas kernels  72 us (46%)
  starting transfers between devices  24.7 us (16%)
  waiting for transfers between devices  15.9 us (10%)
  blocking collectives  14.7 us (9%)
  between operations  14.1 us (9%)
  matrix products  8.44 us (5%)
  local copies, waits for them, and re-layouts  3 us (2%)
    all_to_all x1, blocking collectives, shards(): lax.all_to_all(scan(mine, mine, inner, False), SEQ, 0, 0, tiled=True)  14.7 us
    pallas_call x1, Pallas kernels, shards(): call(backward_kernel, [wide, wide, wide, wide, top, row, col, mat, mat, a...  14.2 us
    pallas_call x1, Pallas kernels, shards(): call(middle_kernel, [pl.BlockSpec((length, cot.shape[1]), lambda i: (0, 0...  14.1 us
    pallas_call x1, Pallas kernels, shards(): call(output_kernel, [pl.BlockSpec((length, width), lambda i: (0, 0)), pl....  8.88 us
    pallas_call x1, Pallas kernels, shards(): call(carry_kernel, [wide, top, wide, wide, col, mat, mat], [wide, top, co...  8.84 us
    all_to_all x1, waiting for transfers between devices, shards(): pieces = lax.all_to_all(part, SEQ, 0, 0, tiled=True)  8.68 us
    dot_general x1, matrix products, dot(): lax.dot_general(a, b, dims, precision=precision, preferred_element_type=F32)  8.44 us
    all_to_all x1, starting transfers between devices, shards(): mine = lax.all_to_all(own, SEQ, 0, 0, tiled=True)  7.96 us
  transfers between devices with their start and end apart: 6, of which 3 were waited for; matrix products, arithmetic and copies ran while one was open for 6% of the time, Pallas kernels for 47%

profile of v1, /device:TPU:0, one launch (start us, length us, event | category | flops | bytes accessed | tf_op | source)
XLA Modules:
  0.0 153.7 jit_solution(6090438679678546634)
XLA Ops:
  7.2 0.0 all-gather.2.cloned.1.call-start
  7.2 0.7 all-gather.2.cloned.1.call-update
  7.9 1.4 reshape_squeeze.3.ld_ref
  9.3 7.4 %shard_map.118 = (f32[4,4,512]{2,1,0:T(4,128)}, f32[4,512,4]{2,1,0:T(8,128)}, bf16[16,128,128]{2,1,0:T(8,128)(2,1)}, bf16[16,144,128]{2,1,0:T(8,128)(2,1)}) custom-call(f32[4,4,512]{2,1,0:T(4,128)} %reshape_squeeze.3.ld_ref, bf16[512,2048]{1,0:T(8,128)(2,1)} %bitcast.23, bf16[512,2048]{1,0:T(8,128)(2,1)} %bitcast.27), custom_call_target="tpu_custom_call" | custom-call | flops 3000000000 | bytes 12500000 | tf_op jit(solution)/shard_map/pallas_call | solution.py:263
  16.7 8.0 %all-to-all-start = ((bf16[16,144,128]{2,1,0:T(8,128)(2,1)}), bf16[16,144,128]{2,1,0:T(8,128)(2,1)S(1)}, u32[]{:S(2)}, u32[]{:S(2)}) async-start(bf16[16,144,128]{2,1,0:T(8,128)(2,1)} %get-tuple-element.31), calls=%async_computation | async-start | bytes 1179648 | tf_op jit(solution)/shard_map/all_to_all | solution.py:278
  24.7 0.0 reduce-scatter.2.cloned.1.call-start
  24.7 6.9 %shard_map.119 = (bf16[512,2048]{1,0:T(8,128)(2,1)}, f32[16,2048]{1,0:T(8,128)}) custom-call(bf16[512,2048]{1,0:T(8,128)(2,1)} %bitcast.19, bf16[512,2048]{1,0:T(8,128)(2,1)} %bitcast.24, bf16[512,2048]{1,0:T(8,128)(2,1)} %bitcast.28, f32[4,4,512]{2,1,0:T(4,128)} %get-tuple-element.27.row_ref, f32[4,512,4]{2,1,0:T(8,128)} %get-tuple-element.28.col_ref), custom_call_target="tpu_custom_call" | custom-call | flops 5400000000 | bytes 22500000 | tf_op jit(solution)/shard_map/pallas_call | solution.py:279
  31.7 5.2 %all-to-all-done.parts_ref.decay_ref = bf16[16,144,128]{2,1,0:T(8,128)(2,1)S(1)} async-done(((bf16[16,144,128]{2,1,0:T(8,128)(2,1)}), bf16[16,144,128]{2,1,0:T(8,128)(2,1)S(1)}, u32[]{:S(2)}, u32[]{:S(2)}) %all-to-all-start) | async-done | bytes 589856 | tf_op jit(solution)/shard_map/all_to_all | solution.py:278
  36.9 0.0 copy-start
  36.9 0.8 copy-done
  37.7 2.2 %shard_map.120 = bf16[16,128,128]{2,1,0:T(8,128)(2,1)} custom-call(bf16[16,144,128]{2,1,0:T(8,128)(2,1)} %copy-done, bf16[16,144,128]{2,1,0:T(8,128)(2,1)} %copy-done, bf16[512,2048]{1,0:T(8,128)(2,1)} %get-tuple-element.29.ordered_ref.inner_ref), custom_call_target="tpu_custom_call" | custom-call | tf_op jit(solution)/shard_map/pallas_call | solution.py:271
  39.9 14.7 %all_to_all.29.in_ref = bf16[16,128,128]{2,1,0:T(8,128)(2,1)} all-to-all(bf16[16,128,128]{2,1,0:T(8,128)(2,1)} %shard_map.120), channel_id=1, replica_groups=mesh['y'=4,'core'=2,'z'=4,'x'=4] {'z','x'}, dimensions={0} | all-to-all | bytes 1048576 | tf_op jit(solution)/shard_map/all_to_all | solution.py:282
  54.6 0.0 copy-start.3
  54.6 8.8 %shard_map.121 = (bf16[512,2048]{1,0:T(8,128)(2,1)}, f32[16,2048]{1,0:T(8,128)}, f32[4,512,4]{2,1,0:T(8,128)}, bf16[512,2048]{1,0:T(8,128)(2,1)}) custom-call(bf16[512,2048]{1,0:T(8,128)(2,1)} %get-tuple-element.29.ordered_ref.inner_ref, f32[16,2048]{1,0:T(8,128)} %get-tuple-element.30.top_ref, bf16[512,2048]{1,0:T(8,128)(2,1)} %bitcast.20, ...), custom_call_target="tpu_custom_call" | custom-call | flops 3000000000 | bytes 12500000 | tf_op jit(solution)/shard_map/pallas_call | solution.py:284
  63.4 0.0 copy-done.3
  63.4 8.4 %convolution_convert_fusion = bf16[2048,2048]{1,0:T(8,128)(2,1)} fusion(bf16[512,2048]{1,0:T(8,128)(2,1)} %get-tuple-element.33.hidden_ref, bf16[1,512,2048]{2,1,0:T(8,128)(2,1)S(1)} %copy-done.3), kind=kOutput, calls=%fused_computation | convolution fusion | flops 4299161600 | bytes 12582912 | tf_op jit(solution)/shard_map/dot_general | solution.py:29
  71.9 0.0 reduce-scatter.2.cloned.1.call-update
  71.9 0.0 all-gather.2.cloned.1.call-done.weight_ref
  71.9 14.1 %shard_map.122 = (bf16[512,2048]{1,0:T(8,128)(2,1)}, bf16[512,2048]{1,0:T(8,128)(2,1)}, bf16[16,2048]{1,0:T(8,128)(2,1)}, bf16[16,128,128]{2,1,0:T(8,128)(2,1)}, bf16[16,128,128]{2,1,0:T(8,128)(2,1)}) custom-call(bf16[512,2048]{1,0:T(8,128)(2,1)} %bitcast.18, bf16[2048,2048]{1,0:T(8,128)(2,1)} %all-gather.2.cloned.1.call-done.weight_ref, ...), custom_call_target="tpu_custom_call" | custom-call | flops 7200000000 | bytes 30000000 | tf_op jit(solution)/shard_map/pallas_call | solution.py:294
  86.1 3.6 %all-to-all-start.2 = ((bf16[16,128,128]{2,1,0:T(8,128)(2,1)}), bf16[16,128,128]{2,1,0:T(8,128)(2,1)S(1)}, u32[]{:S(2)}, u32[]{:S(2)}) async-start(bf16[16,128,128]{2,1,0:T(8,128)(2,1)} %get-tuple-element.37.ordered_ref), calls=%async_computation.2 | async-start | bytes 1048576 | tf_op jit(solution)/shard_map/all_to_all | solution.py:310
  89.6 8.9 %shard_map.123.ordered_ref = bf16[512,2048]{1,0:T(8,128)(2,1)} custom-call(bf16[512,2048]{1,0:T(8,128)(2,1)} %get-tuple-element.33.hidden_ref, bf16[2048,2048]{1,0:T(8,128)(2,1)} %all-gather.2.cloned.1.call-done.weight_ref, bf16[16,128,128]{2,1,0:T(8,128)(2,1)} %get-tuple-element.37.ordered_ref), custom_call_target="tpu_custom_call" | custom-call | flops 4800000000 | bytes 20000000 | tf_op jit(solution)/shard_map/pallas_call | solution.py:311
  98.5 1.2 all-to-all-done.2.parts_ref
  99.7 0.0 copy-start.1
  99.7 0.8 copy-done.1
  100.5 2.2 %shard_map.124.ordered_ref = bf16[16,128,128]{2,1,0:T(8,128)(2,1)} custom-call(bf16[16,128,128]{2,1,0:T(8,128)(2,1)} %copy-done.1, bf16[16,144,128]{2,1,0:T(8,128)(2,1)} %copy-done, bf16[512,2048]{1,0:T(8,128)(2,1)} %shard_map.123.ordered_ref), custom_call_target="tpu_custom_call" | custom-call | tf_op jit(solution)/shard_map/pallas_call | solution.py:271
  102.8 5.9 %all-to-all-start.3 = ((bf16[16,128,128]{2,1,0:T(8,128)(2,1)}), bf16[16,128,128]{2,1,0:T(8,128)(2,1)S(1)}, u32[]{:S(2)}, u32[]{:S(2)}) async-start(bf16[16,128,128]{2,1,0:T(8,128)(2,1)} %shard_map.124.ordered_ref), calls=%async_computation.3 | async-start | bytes 1048576 | tf_op jit(solution)/shard_map/all_to_all | solution.py:323
  108.7 14.2 %shard_map.125 = (bf16[512,2048]{1,0:T(8,128)(2,1)}, bf16[512,2048]{1,0:T(8,128)(2,1)}, bf16[512,2048]{1,0:T(8,128)(2,1)}) custom-call(bf16[512,2048]{1,0:T(8,128)(2,1)} %bitcast.22, bf16[512,2048]{1,0:T(8,128)(2,1)} %bitcast.25, bf16[512,2048]{1,0:T(8,128)(2,1)} %bitcast.29, bf16[512,2048]{1,0:T(8,128)(2,1)} %get-tuple-element.38.dm_ref, ...), custom_call_target="tpu_custom_call" | custom-call | flops 7800000000 | bytes 32500000 | tf_op jit(solution)/shard_map/pallas_call | solution.py:324
  122.9 0.0 reduce-scatter.2.cloned.1.call-done
  122.9 0.0 all-to-all-done.3.ret_ref
  122.9 0.0 copy-start.2
  122.9 7.2 %all-to-all-start.4 = ((bf16[16,16,2048]{2,1,0:T(8,128)(2,1)}), bf16[16,16,2048]{2,1,0:T(8,128)(2,1)S(1)}, u32[]{:S(2)}, u32[]{:S(2)}) async-start(bf16[16,16,2048]{2,1,0:T(8,128)(2,1)} %bitcast.15), calls=%async_computation.5 | async-start | bytes 2097152 | tf_op jit(solution)/shard_map/all_to_all | solution.py:337
  130.1 0.0 copy-done.2
  130.1 7.2 %shard_map.126 = (bf16[512,2048]{1,0:T(8,128)(2,1)}, bf16[512,2048]{1,0:T(8,128)(2,1)}) custom-call(bf16[512,2048]{1,0:T(8,128)(2,1)} %bitcast.26, bf16[512,2048]{1,0:T(8,128)(2,1)} %bitcast.30, bf16[512,2048]{1,0:T(8,128)(2,1)} %get-tuple-element.41.pk_ref, bf16[512,2048]{1,0:T(8,128)(2,1)} %get-tuple-element.42.pv_ref, ...), custom_call_target="tpu_custom_call" | custom-call | flops 3000000000 | bytes 12500000 | tf_op jit(solution)/shard_map/pallas_call | solution.py:331
  137.3 8.7 %all-to-all-done.4 = bf16[16,16,2048]{2,1,0:T(8,128)(2,1)S(1)} async-done(((bf16[16,16,2048]{2,1,0:T(8,128)(2,1)}), bf16[16,16,2048]{2,1,0:T(8,128)(2,1)S(1)}, u32[]{:S(2)}, u32[]{:S(2)}) %all-to-all-start.4) | async-done | bytes 1048608 | tf_op jit(solution)/shard_map/all_to_all | solution.py:337
  146.0 0.1 convert_reduce_fusion
  146.1 0.7 broadcast_multiply_fusion
Async XLA Ops:
  7.2 64.8 %all-gather.2.cloned.1.call-start = ((), (), s32[]{:S(2)}) async-start(), calls=%async_computation.6 | async-start | bytes 9437184 | tf_op jit(solution)/shard_map/all_gather | solution.py:262
  16.7 20.2 %all-to-all-start = ((bf16[16,144,128]{2,1,0:T(8,128)(2,1)}), bf16[16,144,128]{2,1,0:T(8,128)(2,1)S(1)}, u32[]{:S(2)}, u32[]{:S(2)}) async-start(bf16[16,144,128]{2,1,0:T(8,128)(2,1)} %get-tuple-element.31), calls=%async_computation | async-start | bytes 1179648 | tf_op jit(solution)/shard_map/all_to_all | solution.py:278
  24.7 98.2 %reduce-scatter.2.cloned.1.call-start = ((), (), s32[]{:S(2)}) async-start(), calls=%async_computation.7 | async-start | bytes 9437184 | tf_op jit(solution)/shard_map/reduce_scatter | solution.py:292
  36.9 0.8 copy-start
  54.6 8.8 %copy-start.3 = (bf16[1,512,2048]{2,1,0:T(8,128)(2,1)S(1)}, bf16[1,512,2048]{2,1,0:T(8,128)(2,1)}, u32[]{:S(2)}) copy-start(bf16[1,512,2048]{2,1,0:T(8,128)(2,1)} %param.13) | copy-start | bytes 6291460
  86.1 13.7 %all-to-all-start.2 = ((bf16[16,128,128]{2,1,0:T(8,128)(2,1)}), bf16[16,128,128]{2,1,0:T(8,128)(2,1)S(1)}, u32[]{:S(2)}, u32[]{:S(2)}) async-start(bf16[16,128,128]{2,1,0:T(8,128)(2,1)} %get-tuple-element.37.ordered_ref), calls=%async_computation.2 | async-start | bytes 1048576 | tf_op jit(solution)/shard_map/all_to_all | solution.py:310
  99.7 0.8 copy-start.1
  102.8 20.1 %all-to-all-start.3 = ((bf16[16,128,128]{2,1,0:T(8,128)(2,1)}), bf16[16,128,128]{2,1,0:T(8,128)(2,1)S(1)}, u32[]{:S(2)}, u32[]{:S(2)}) async-start(bf16[16,128,128]{2,1,0:T(8,128)(2,1)} %shard_map.124.ordered_ref), calls=%async_computation.3 | async-start | bytes 1048576 | tf_op jit(solution)/shard_map/all_to_all | solution.py:323
  122.9 7.2 %copy-start.2 = (bf16[16,128,128]{2,1,0:T(8,128)(2,1)}, bf16[16,128,128]{2,1,0:T(8,128)(2,1)S(1)}, u32[]{:S(2)}) copy-start(bf16[16,128,128]{2,1,0:T(8,128)(2,1)S(1)} %all-to-all-done.3.ret_ref) | copy-start | bytes 1572868
  122.9 23.1 %all-to-all-start.4 = ((bf16[16,16,2048]{2,1,0:T(8,128)(2,1)}), bf16[16,16,2048]{2,1,0:T(8,128)(2,1)S(1)}, u32[]{:S(2)}, u32[]{:S(2)}) async-start(bf16[16,16,2048]{2,1,0:T(8,128)(2,1)} %bitcast.15), calls=%async_computation.5 | async-start | bytes 2097152 | tf_op jit(solution)/shard_map/all_to_all | solution.py:337
Sparse Core Ops, SparseCore 0:
  9.7 52.1 all-gather.1
  72.0 50.0 reduce-scatter.1

commit v2 on v1

--- a/solution.py
+++ b/solution.py
@@ -48,10 +48,13 @@
 
 def states_kernel(ld_ref, k_ref, v_ref, row_ref, col_ref, first_ref, own_ref):
     chunks = ld_ref.shape[2] // CHUNK
+    step = pl.program_id(0)
+    pair = pl.ds(pl.multiple_of(step // 2 * 2 * GROUP, 2 * GROUP), 2 * GROUP)
     lower = jnp.where(causal((CHUNK, CHUNK)), 1.0, 0.0).astype(F32)
     for c in range(chunks):
         t = slice(c * CHUNK, (c + 1) * CHUNK)
-        part = ld_ref[0, :, t]
+        both = ld_ref[0, pair, t]
+        part = jnp.where(step % 2 == 0, both[:GROUP], both[GROUP:])
         row_ref[0, :, t] = dot(part, lower, NT, HIGHEST)
         col_ref[0, t, :] = dot(lower, part, NT, HIGHEST)
     for h in range(GROUP):
@@ -97,7 +100,9 @@
     return 0.5 + 0.5 * jnp.tanh(0.5 * x)
 
 
-def inner_kernel(q_ref, k_ref, v_ref, row_ref, col_ref, inner_ref, top_ref):
+def inner_kernel(
+    q_ref, k_ref, v_ref, g_ref, row_ref, col_ref, inner_ref, top_ref, silu_ref
+):
     chunks = q_ref.shape[0] // CHUNK
     for h in range(GROUP):
         w = slice(h * HEAD, (h + 1) * HEAD)
@@ -105,6 +110,8 @@
             t = slice(c * CHUNK, (c + 1) * CHUNK)
             _, weights = decays(row_ref, col_ref, h, c)
             scores = (dot(q_ref[t, w], k_ref[t, w], NT) * weights).astype(BF16)
+            gate = g_ref[t, w].astype(F32)
+            silu_ref[t, w] = (gate * sigmoid(gate)).astype(BF16)
             inner = dot(scores, v_ref[t, w], NN)
             inner_ref[t, w] = inner.astype(BF16)
             if c == 0:
@@ -112,8 +119,8 @@
 
 
 def carry_kernel(
-    inner_ref, top_ref, q_ref, g_ref, col_ref, in_ref, first_ref,
-    norm_ref, norm_top_ref, rms_ref, hidden_ref,
+    inner_ref, top_ref, q_ref, silu_ref, col_ref, in_ref, first_ref, cot_ref,
+    norm_ref, norm_top_ref, rms_ref, hidden_ref, partial_ref,
 ):
     chunks = q_ref.shape[0] // CHUNK
     for h in range(GROUP):
@@ -131,12 +138,14 @@
                 state = (state.astype(F32) * end + first_ref[h].astype(F32)).astype(BF16)
             rms = lax.rsqrt(jnp.mean(mixed * mixed, axis=-1, keepdims=True) + 1e-05)
             normal = mixed * rms
-            gate = g_ref[t, w].astype(F32)
             norm_ref[t, w] = normal.astype(BF16)
             if c == 0:
                 norm_top_ref[:, w] = normal[:TOP]
             rms_ref[0, t, h : h + 1] = rms
-            hidden_ref[t, w] = (normal * (gate * sigmoid(gate))).astype(BF16)
+            hidden_ref[t, w] = (normal * silu_ref[t, w].astype(F32)).astype(BF16)
+        if h % 2 == 1:
+            pair = slice((h - 1) * HEAD, (h + 1) * HEAD)
+            partial_ref[pair, :] = dot(hidden_ref[:, pair], cot_ref[...], TN).astype(BF16)
 
 
 def middle_kernel(
@@ -230,9 +239,9 @@
     heads = log_decay.shape[1]
     groups = heads // GROUP
     q, k, v, g, cot = (a[0] for a in (queries, keys, values, gates, grad_out))
-    ld = log_decay[0].reshape(groups, GROUP, length)
 
     wide = pl.BlockSpec((length, GROUP * HEAD), lambda i: (0, i))
+    all_decays = pl.BlockSpec((1, heads, length), lambda i: (0, 0, 0))
     top = pl.BlockSpec((TOP, GROUP * HEAD), lambda i: (0, i))
     row = pl.BlockSpec((1, GROUP, length), lambda i: (i, 0, 0))
     col = pl.BlockSpec((1, length, GROUP), lambda i: (i, 0, 0))
@@ -261,8 +270,8 @@
 
     whole = lax.all_gather(out_weight, FSDP, axis=0, tiled=True)
     a_row, a_col, first, own = call(
-        states_kernel, [row, wide, wide], [row, col, mat, message], [row_t, col_t, mat_t, message_t]
-    )(ld, k, v)
+        states_kernel, [all_decays, wide, wide], [row, col, mat, message], [row_t, col_t, mat_t, message_t]
+    )(log_decay, k, v)
 
     anywhere = pl.BlockSpec(memory_space=pl.ANY)
     vmem = pl.BlockSpec(memory_space=pltpu.VMEM)
@@ -276,19 +285,29 @@
         )(parts, decay, ordered)
 
     mine = lax.all_to_all(own, SEQ, 0, 0, tiled=True)
-    inner, inner_top = call(
-        inner_kernel, [wide, wide, wide, row, col], [wide, top], [wide_t, top_f], us=9
-    )(q, k, v, a_row, a_col)
+    inner, inner_top, silu = call(
+        inner_kernel,
+        [wide, wide, wide, wide, row, col],
+        [wide, top, wide],
+        [wide_t, top_f, wide_t],
+        us=9,
+    )(q, k, v, g, a_row, a_col)
     incoming = lax.all_to_all(scan(mine, mine, inner, False), SEQ, 0, 0, tiled=True)
 
-    normal, normal_top, rms, hidden = call(
+    normal, normal_top, rms, hidden, partial_grad = call(
         carry_kernel,
-        [wide, top, wide, wide, col, mat, mat],
-        [wide, top, col, wide],
-        [wide_t, top_f, col_t, wide_t],
-    )(inner, inner_top, q, g, a_col, incoming, first)
-
-    partial_grad = dot(hidden, cot, TN).astype(BF16)
+        [wide, top, wide, wide, col, mat, mat, pl.BlockSpec(cot.shape, lambda i: (0, 0))],
+        [wide, top, col, wide, pl.BlockSpec((GROUP * HEAD, cot.shape[1]), lambda i: (i, 0))],
+        [
+            wide_t,
+            top_f,
+            col_t,
+            wide_t,
+            jax.ShapeDtypeStruct((width, cot.shape[1]), BF16),
+        ],
+        us=12,
+    )(inner, inner_top, q, silu, a_col, incoming, first, cot)
+
     part = lax.psum_scatter(partial_grad, FSDP, scatter_dimension=0, tiled=True)
 
     grad_gate, dm, dm_low, last, later = call(

time: 155 us -> 150 us (0.968)
  matrix products: 8.44 us -> 0 us
  Pallas kernels: 72 us -> 77.9 us
    dot_general x1 -> x0, matrix products: 8.44 us -> none  [dot(): lax.dot_general(a, b, dims, precision=precision, preferred_element_type=F32)]
    pallas_call x3, Pallas kernels: 23.2 us -> 28.8 us  [the longest x1 13.1 us: shards(): call(carry_kernel, [wide, top, wide, wide, col, mat, mat, pl.BlockSpec(co...]
  transfers between devices with their start and end apart: 6 -> 6, of which waited for: 3 -> 3; matrix products, arithmetic and copies ran while one was open for 6% -> 0% of each run, Pallas kernels for 47% -> 52%
where the time goes in v2:
time: 150 us; the launch traced here: 149 us
  Pallas kernels  77.9 us (52%)
  starting transfers between devices  24.4 us (16%)
  waiting for transfers between devices  15.1 us (10%)
  blocking collectives  14.6 us (10%)
  between operations  14.1 us (9%)
  local copies, waits for them, and re-layouts  1.62 us (1%)
    all_to_all x1, blocking collectives, shards(): lax.all_to_all(scan(mine, mine, inner, False), SEQ, 0, 0, tiled=True)  14.6 us
    pallas_call x1, Pallas kernels, shards(): call(middle_kernel, [pl.BlockSpec((length, cot.shape[1]), lambda i: (0, 0...  14.4 us
    pallas_call x1, Pallas kernels, shards(): call(backward_kernel, [wide, wide, wide, wide, top, row, col, mat, mat, a...  14.2 us
    pallas_call x1, Pallas kernels, shards(): call(carry_kernel, [wide, top, wide, wide, col, mat, mat, pl.BlockSpec(co...  13.1 us
    pallas_call x1, Pallas kernels, shards(): call(output_kernel, [pl.BlockSpec((length, width), lambda i: (0, 0)), pl....  8.88 us
    all_to_all x1, waiting for transfers between devices, shards(): pieces = lax.all_to_all(part, SEQ, 0, 0, tiled=True)  8.85 us
    pallas_call x1, Pallas kernels, shards(): call(inner_kernel, [wide, wide, wide, wide, row, col], [wide, top, wide],...  8.26 us
    all_to_all x1, starting transfers between devices, shards(): mine = lax.all_to_all(own, SEQ, 0, 0, tiled=True)  7.96 us
  transfers between devices with their start and end apart: 6, of which 3 were waited for; matrix products, arithmetic and copies ran while one was open for 0% of the time, Pallas kernels for 52%

profile of v2, /device:TPU:0, one launch (start us, length us, event | category | flops | bytes accessed | tf_op | source)
XLA Modules:
  0.0 148.6 jit_solution(15741138615399195325)
XLA Ops:
  7.2 0.0 all-gather.2.cloned.1.call-start
  7.2 0.7 all-gather.2.cloned.1.call-update
  7.9 7.4 %shard_map.118 = (f32[4,4,512]{2,1,0:T(4,128)}, f32[4,512,4]{2,1,0:T(8,128)}, bf16[16,128,128]{2,1,0:T(8,128)(2,1)}, bf16[16,144,128]{2,1,0:T(8,128)(2,1)}) custom-call(f32[1,16,512]{2,1,0:T(8,128)} %ld_ref.1, bf16[512,2048]{1,0:T(8,128)(2,1)} %bitcast.21, bf16[512,2048]{1,0:T(8,128)(2,1)} %bitcast.25), custom_call_target="tpu_custom_call" | custom-call | flops 3000000000 | bytes 12500000 | tf_op jit(solution)/shard_map/pallas_call | solution.py:272
  15.3 8.0 %all-to-all-start = ((bf16[16,144,128]{2,1,0:T(8,128)(2,1)}), bf16[16,144,128]{2,1,0:T(8,128)(2,1)S(1)}, u32[]{:S(2)}, u32[]{:S(2)}) async-start(bf16[16,144,128]{2,1,0:T(8,128)(2,1)} %get-tuple-element.34), calls=%async_computation | async-start | bytes 1179648 | tf_op jit(solution)/shard_map/all_to_all | solution.py:287
  23.3 0.0 reduce-scatter.2.cloned.1.call-start
  23.3 8.3 %shard_map.119 = (bf16[512,2048]{1,0:T(8,128)(2,1)}, f32[16,2048]{1,0:T(8,128)}, bf16[512,2048]{1,0:T(8,128)(2,1)}) custom-call(bf16[512,2048]{1,0:T(8,128)(2,1)} %bitcast.17, bf16[512,2048]{1,0:T(8,128)(2,1)} %bitcast.22, bf16[512,2048]{1,0:T(8,128)(2,1)} %bitcast.26, bf16[512,2048]{1,0:T(8,128)(2,1)} %bitcast.13, f32[4,4,512]{2,1,0:T(4,128)} %get-tuple-element.29.row_ref, ...), custom_call_target="tpu_custom_call" | custom-call | flops 5400000000 | bytes 22500000 | tf_op jit(solution)/shard_map/pallas_call | solution.py:288
  31.6 3.9 %all-to-all-done.parts_ref.decay_ref = bf16[16,144,128]{2,1,0:T(8,128)(2,1)S(1)} async-done(((bf16[16,144,128]{2,1,0:T(8,128)(2,1)}), bf16[16,144,128]{2,1,0:T(8,128)(2,1)S(1)}, u32[]{:S(2)}, u32[]{:S(2)}) %all-to-all-start) | async-done | bytes 589856 | tf_op jit(solution)/shard_map/all_to_all | solution.py:287
  35.5 0.0 copy-start
  35.5 0.8 copy-done
  36.3 2.2 %shard_map.120 = bf16[16,128,128]{2,1,0:T(8,128)(2,1)} custom-call(bf16[16,144,128]{2,1,0:T(8,128)(2,1)} %copy-done, bf16[16,144,128]{2,1,0:T(8,128)(2,1)} %copy-done, bf16[512,2048]{1,0:T(8,128)(2,1)} %get-tuple-element.31.ordered_ref.inner_ref), custom_call_target="tpu_custom_call" | custom-call | tf_op jit(solution)/shard_map/pallas_call | solution.py:280
  38.5 14.6 %all_to_all.29.in_ref = bf16[16,128,128]{2,1,0:T(8,128)(2,1)} all-to-all(bf16[16,128,128]{2,1,0:T(8,128)(2,1)} %shard_map.120), channel_id=1, replica_groups=mesh['y'=4,'core'=2,'z'=4,'x'=4] {'z','x'}, dimensions={0} | all-to-all | bytes 1048576 | tf_op jit(solution)/shard_map/all_to_all | solution.py:295
  53.2 13.1 %shard_map.121 = (bf16[512,2048]{1,0:T(8,128)(2,1)}, f32[16,2048]{1,0:T(8,128)}, f32[4,512,4]{2,1,0:T(8,128)}, bf16[512,2048]{1,0:T(8,128)(2,1)}, bf16[2048,2048]{1,0:T(8,128)(2,1)}) custom-call(bf16[512,2048]{1,0:T(8,128)(2,1)} %get-tuple-element.31.ordered_ref.inner_ref, f32[16,2048]{1,0:T(8,128)} %get-tuple-element.32.top_ref, ...), custom_call_target="tpu_custom_call" | custom-call | flops 7200000000 | bytes 30000000 | tf_op jit(solution)/shard_map/pallas_call | solution.py:297
  66.3 0.0 reduce-scatter.2.cloned.1.call-update
  66.3 0.0 all-gather.2.cloned.1.call-done.weight_ref
  66.4 14.4 %shard_map.122 = (bf16[512,2048]{1,0:T(8,128)(2,1)}, bf16[512,2048]{1,0:T(8,128)(2,1)}, bf16[16,2048]{1,0:T(8,128)(2,1)}, bf16[16,128,128]{2,1,0:T(8,128)(2,1)}, bf16[16,128,128]{2,1,0:T(8,128)(2,1)}) custom-call(bf16[512,2048]{1,0:T(8,128)(2,1)} %bitcast.16, bf16[2048,2048]{1,0:T(8,128)(2,1)} %all-gather.2.cloned.1.call-done.weight_ref, ...), custom_call_target="tpu_custom_call" | custom-call | flops 7200000000 | bytes 30000000 | tf_op jit(solution)/shard_map/pallas_call | solution.py:313
  80.8 3.6 %all-to-all-start.2 = ((bf16[16,128,128]{2,1,0:T(8,128)(2,1)}), bf16[16,128,128]{2,1,0:T(8,128)(2,1)S(1)}, u32[]{:S(2)}, u32[]{:S(2)}) async-start(bf16[16,128,128]{2,1,0:T(8,128)(2,1)} %get-tuple-element.40.ordered_ref), calls=%async_computation.2 | async-start | bytes 1048576 | tf_op jit(solution)/shard_map/all_to_all | solution.py:329
  84.4 8.9 %shard_map.123.ordered_ref = bf16[512,2048]{1,0:T(8,128)(2,1)} custom-call(bf16[512,2048]{1,0:T(8,128)(2,1)} %get-tuple-element.36.hidden_ref, bf16[2048,2048]{1,0:T(8,128)(2,1)} %all-gather.2.cloned.1.call-done.weight_ref, bf16[16,128,128]{2,1,0:T(8,128)(2,1)} %get-tuple-element.40.ordered_ref), custom_call_target="tpu_custom_call" | custom-call | flops 4800000000 | bytes 20000000 | tf_op jit(solution)/shard_map/pallas_call | solution.py:330
  93.2 1.5 %all-to-all-done.2.parts_ref = bf16[16,128,128]{2,1,0:T(8,128)(2,1)S(1)} async-done(((bf16[16,128,128]{2,1,0:T(8,128)(2,1)}), bf16[16,128,128]{2,1,0:T(8,128)(2,1)S(1)}, u32[]{:S(2)}, u32[]{:S(2)}) %all-to-all-start.2) | async-done | bytes 524320 | tf_op jit(solution)/shard_map/all_to_all | solution.py:329
  94.8 0.0 copy-start.1
  94.8 0.8 copy-done.1
  95.6 2.2 %shard_map.124.ordered_ref = bf16[16,128,128]{2,1,0:T(8,128)(2,1)} custom-call(bf16[16,128,128]{2,1,0:T(8,128)(2,1)} %copy-done.1, bf16[16,144,128]{2,1,0:T(8,128)(2,1)} %copy-done, bf16[512,2048]{1,0:T(8,128)(2,1)} %shard_map.123.ordered_ref), custom_call_target="tpu_custom_call" | custom-call | tf_op jit(solution)/shard_map/pallas_call | solution.py:280
  97.8 5.6 %all-to-all-start.3 = ((bf16[16,128,128]{2,1,0:T(8,128)(2,1)}), bf16[16,128,128]{2,1,0:T(8,128)(2,1)S(1)}, u32[]{:S(2)}, u32[]{:S(2)}) async-start(bf16[16,128,128]{2,1,0:T(8,128)(2,1)} %shard_map.124.ordered_ref), calls=%async_computation.3 | async-start | bytes 1048576 | tf_op jit(solution)/shard_map/all_to_all | solution.py:342
  103.4 14.2 %shard_map.125 = (bf16[512,2048]{1,0:T(8,128)(2,1)}, bf16[512,2048]{1,0:T(8,128)(2,1)}, bf16[512,2048]{1,0:T(8,128)(2,1)}) custom-call(bf16[512,2048]{1,0:T(8,128)(2,1)} %bitcast.20, bf16[512,2048]{1,0:T(8,128)(2,1)} %bitcast.23, bf16[512,2048]{1,0:T(8,128)(2,1)} %bitcast.27, bf16[512,2048]{1,0:T(8,128)(2,1)} %get-tuple-element.41.dm_ref, ...), custom_call_target="tpu_custom_call" | custom-call | flops 7800000000 | bytes 32500000 | tf_op jit(solution)/shard_map/pallas_call | solution.py:343
  117.6 0.0 reduce-scatter.2.cloned.1.call-done
  117.6 0.0 all-to-all-done.3.ret_ref
  117.7 0.0 copy-start.2
  117.7 7.2 %all-to-all-start.4 = ((bf16[16,16,2048]{2,1,0:T(8,128)(2,1)}), bf16[16,16,2048]{2,1,0:T(8,128)(2,1)S(1)}, u32[]{:S(2)}, u32[]{:S(2)}) async-start(bf16[16,16,2048]{2,1,0:T(8,128)(2,1)} %bitcast.12), calls=%async_computation.5 | async-start | bytes 2097152 | tf_op jit(solution)/shard_map/all_to_all | solution.py:356
  124.9 0.0 copy-done.2
  124.9 7.2 %shard_map.126 = (bf16[512,2048]{1,0:T(8,128)(2,1)}, bf16[512,2048]{1,0:T(8,128)(2,1)}) custom-call(bf16[512,2048]{1,0:T(8,128)(2,1)} %bitcast.24, bf16[512,2048]{1,0:T(8,128)(2,1)} %bitcast.28, bf16[512,2048]{1,0:T(8,128)(2,1)} %get-tuple-element.44.pk_ref, bf16[512,2048]{1,0:T(8,128)(2,1)} %get-tuple-element.45.pv_ref, ...), custom_call_target="tpu_custom_call" | custom-call | flops 3000000000 | bytes 12500000 | tf_op jit(solution)/shard_map/pallas_call | solution.py:350
  132.1 8.9 %all-to-all-done.4 = bf16[16,16,2048]{2,1,0:T(8,128)(2,1)S(1)} async-done(((bf16[16,16,2048]{2,1,0:T(8,128)(2,1)}), bf16[16,16,2048]{2,1,0:T(8,128)(2,1)S(1)}, u32[]{:S(2)}, u32[]{:S(2)}) %all-to-all-start.4) | async-done | bytes 1048608 | tf_op jit(solution)/shard_map/all_to_all | solution.py:356
  140.9 0.1 convert_reduce_fusion
  141.1 0.7 broadcast_multiply_fusion
Async XLA Ops:
  7.2 59.2 %all-gather.2.cloned.1.call-start = ((), (), s32[]{:S(2)}) async-start(), calls=%async_computation.6 | async-start | bytes 9437184 | tf_op jit(solution)/shard_map/all_gather | solution.py:271
  15.3 20.2 %all-to-all-start = ((bf16[16,144,128]{2,1,0:T(8,128)(2,1)}), bf16[16,144,128]{2,1,0:T(8,128)(2,1)S(1)}, u32[]{:S(2)}, u32[]{:S(2)}) async-start(bf16[16,144,128]{2,1,0:T(8,128)(2,1)} %get-tuple-element.34), calls=%async_computation | async-start | bytes 1179648 | tf_op jit(solution)/shard_map/all_to_all | solution.py:287
  23.3 94.3 %reduce-scatter.2.cloned.1.call-start = ((), (), s32[]{:S(2)}) async-start(), calls=%async_computation.7 | async-start | bytes 9437184 | tf_op jit(solution)/shard_map/reduce_scatter | solution.py:311
  35.5 0.8 copy-start
  80.8 14.0 %all-to-all-start.2 = ((bf16[16,128,128]{2,1,0:T(8,128)(2,1)}), bf16[16,128,128]{2,1,0:T(8,128)(2,1)S(1)}, u32[]{:S(2)}, u32[]{:S(2)}) async-start(bf16[16,128,128]{2,1,0:T(8,128)(2,1)} %get-tuple-element.40.ordered_ref), calls=%async_computation.2 | async-start | bytes 1048576 | tf_op jit(solution)/shard_map/all_to_all | solution.py:329
  94.8 0.8 copy-start.1
  97.8 19.8 %all-to-all-start.3 = ((bf16[16,128,128]{2,1,0:T(8,128)(2,1)}), bf16[16,128,128]{2,1,0:T(8,128)(2,1)S(1)}, u32[]{:S(2)}, u32[]{:S(2)}) async-start(bf16[16,128,128]{2,1,0:T(8,128)(2,1)} %shard_map.124.ordered_ref), calls=%async_computation.3 | async-start | bytes 1048576 | tf_op jit(solution)/shard_map/all_to_all | solution.py:342
  117.7 7.2 %copy-start.2 = (bf16[16,128,128]{2,1,0:T(8,128)(2,1)}, bf16[16,128,128]{2,1,0:T(8,128)(2,1)S(1)}, u32[]{:S(2)}) copy-start(bf16[16,128,128]{2,1,0:T(8,128)(2,1)S(1)} %all-to-all-done.3.ret_ref) | copy-start | bytes 1572868
  117.7 23.3 %all-to-all-start.4 = ((bf16[16,16,2048]{2,1,0:T(8,128)(2,1)}), bf16[16,16,2048]{2,1,0:T(8,128)(2,1)S(1)}, u32[]{:S(2)}, u32[]{:S(2)}) async-start(bf16[16,16,2048]{2,1,0:T(8,128)(2,1)} %bitcast.12), calls=%async_computation.5 | async-start | bytes 2097152 | tf_op jit(solution)/shard_map/all_to_all | solution.py:356
Sparse Core Ops, SparseCore 0:
  9.7 52.2 all-gather.1
  66.5 50.4 reduce-scatter.1

commit v3 on v2

--- a/solution.py
+++ b/solution.py
@@ -101,14 +101,15 @@
 
 
 def inner_kernel(
-    q_ref, k_ref, v_ref, g_ref, row_ref, col_ref, inner_ref, top_ref, silu_ref
+    q_ref, k_ref, v_ref, g_ref, row_ref, col_ref, inner_ref, top_ref, silu_ref, faded_ref
 ):
     chunks = q_ref.shape[0] // CHUNK
     for h in range(GROUP):
         w = slice(h * HEAD, (h + 1) * HEAD)
         for c in range(chunks):
             t = slice(c * CHUNK, (c + 1) * CHUNK)
-            _, weights = decays(row_ref, col_ref, h, c)
+            a, weights = decays(row_ref, col_ref, h, c)
+            faded_ref[t, w] = (q_ref[t, w].astype(F32) * jnp.exp(a)).astype(BF16)
             scores = (dot(q_ref[t, w], k_ref[t, w], NT) * weights).astype(BF16)
             gate = g_ref[t, w].astype(F32)
             silu_ref[t, w] = (gate * sigmoid(gate)).astype(BF16)
@@ -132,7 +133,7 @@
             inner = inner_ref[t, w].astype(F32)
             if c == 0:
                 inner = jnp.concatenate([top_ref[:, w], inner[TOP:]], axis=0)
-            mixed = inner + dot(q_ref[t, w], state, NN) * jnp.exp(a)
+            mixed = inner + dot(q_ref[t, w], state, NN)
             if c + 1 < chunks:
                 end = jnp.exp(a[CHUNK - 1 : CHUNK])
                 state = (state.astype(F32) * end + first_ref[h].astype(F32)).astype(BF16)
@@ -285,11 +286,11 @@
         )(parts, decay, ordered)
 
     mine = lax.all_to_all(own, SEQ, 0, 0, tiled=True)
-    inner, inner_top, silu = call(
+    inner, inner_top, silu, faded = call(
         inner_kernel,
         [wide, wide, wide, wide, row, col],
-        [wide, top, wide],
-        [wide_t, top_f, wide_t],
+        [wide, top, wide, wide],
+        [wide_t, top_f, wide_t, wide_t],
         us=9,
     )(q, k, v, g, a_row, a_col)
     incoming = lax.all_to_all(scan(mine, mine, inner, False), SEQ, 0, 0, tiled=True)
@@ -306,7 +307,7 @@
             jax.ShapeDtypeStruct((width, cot.shape[1]), BF16),
         ],
         us=12,
-    )(inner, inner_top, q, silu, a_col, incoming, first, cot)
+    )(inner, inner_top, faded, silu, a_col, incoming, first, cot)
 
     part = lax.psum_scatter(partial_grad, FSDP, scatter_dimension=0, tiled=True)
 

time: 150 us -> 150 us (level)
  transfers between devices with their start and end apart: 6 -> 6, of which waited for: 3 -> 3; matrix products, arithmetic and copies ran while one was open for 0% -> 0% of each run, Pallas kernels for 52% -> 53%
where the time goes in v3:
time: 150 us; the launch traced here: 149 us
  Pallas kernels  78.1 us (52%)
  starting transfers between devices  24.5 us (16%)
  blocking collectives  14.9 us (10%)
  waiting for transfers between devices  14.5 us (10%)
  between operations  14.1 us (9%)
  local copies, waits for them, and re-layouts  1.65 us (1%)
    all_to_all x1, blocking collectives, shards(): lax.all_to_all(scan(mine, mine, inner, False), SEQ, 0, 0, tiled=True)  14.9 us
    pallas_call x1, Pallas kernels, shards(): call(middle_kernel, [pl.BlockSpec((length, cot.shape[1]), lambda i: (0, 0...  14.5 us
    pallas_call x1, Pallas kernels, shards(): call(backward_kernel, [wide, wide, wide, wide, top, row, col, mat, mat, a...  14.2 us
    pallas_call x1, Pallas kernels, shards(): call(carry_kernel, [wide, top, wide, wide, col, mat, mat, pl.BlockSpec(co...  12.8 us
    pallas_call x1, Pallas kernels, shards(): call(output_kernel, [pl.BlockSpec((length, width), lambda i: (0, 0)), pl....  8.88 us
    all_to_all x1, waiting for transfers between devices, shards(): pieces = lax.all_to_all(part, SEQ, 0, 0, tiled=True)  8.85 us
    pallas_call x1, Pallas kernels, shards(): call(inner_kernel, [wide, wide, wide, wide, row, col], [wide, top, wide,...  8.8 us
    all_to_all x1, starting transfers between devices, shards(): mine = lax.all_to_all(own, SEQ, 0, 0, tiled=True)  7.96 us
  transfers between devices with their start and end apart: 6, of which 3 were waited for; matrix products, arithmetic and copies ran while one was open for 0% of the time, Pallas kernels for 53%

profile of v3, /device:TPU:0, one launch (start us, length us, event | category | flops | bytes accessed | tf_op | source)
XLA Modules:
  0.0 148.6 jit_solution(7616116626925779575)
XLA Ops:
  7.2 0.0 all-gather.2.cloned.1.call-start
  7.2 0.7 all-gather.2.cloned.1.call-update
  7.9 7.4 %shard_map.118 = (f32[4,4,512]{2,1,0:T(4,128)}, f32[4,512,4]{2,1,0:T(8,128)}, bf16[16,128,128]{2,1,0:T(8,128)(2,1)}, bf16[16,144,128]{2,1,0:T(8,128)(2,1)}) custom-call(f32[1,16,512]{2,1,0:T(8,128)} %ld_ref.1, bf16[512,2048]{1,0:T(8,128)(2,1)} %bitcast.20, bf16[512,2048]{1,0:T(8,128)(2,1)} %bitcast.24), custom_call_target="tpu_custom_call" | custom-call | flops 3000000000 | bytes 12500000 | tf_op jit(solution)/shard_map/pallas_call | solution.py:273
  15.3 8.0 %all-to-all-start = ((bf16[16,144,128]{2,1,0:T(8,128)(2,1)}), bf16[16,144,128]{2,1,0:T(8,128)(2,1)S(1)}, u32[]{:S(2)}, u32[]{:S(2)}) async-start(bf16[16,144,128]{2,1,0:T(8,128)(2,1)} %get-tuple-element.36), calls=%async_computation | async-start | bytes 1179648 | tf_op jit(solution)/shard_map/all_to_all | solution.py:288
  23.3 0.0 reduce-scatter.2.cloned.1.call-start
  23.3 8.8 %shard_map.119 = (bf16[512,2048]{1,0:T(8,128)(2,1)}, f32[16,2048]{1,0:T(8,128)}, bf16[512,2048]{1,0:T(8,128)(2,1)}, bf16[512,2048]{1,0:T(8,128)(2,1)}) custom-call(bf16[512,2048]{1,0:T(8,128)(2,1)} %bitcast.17, bf16[512,2048]{1,0:T(8,128)(2,1)} %bitcast.21, bf16[512,2048]{1,0:T(8,128)(2,1)} %bitcast.25, bf16[512,2048]{1,0:T(8,128)(2,1)} %bitcast.13, ...), custom_call_target="tpu_custom_call" | custom-call | flops 5400000000 | bytes 22500000 | tf_op jit(solution)/shard_map/pallas_call | solution.py:289
  32.1 3.4 %all-to-all-done.parts_ref.decay_ref = bf16[16,144,128]{2,1,0:T(8,128)(2,1)S(1)} async-done(((bf16[16,144,128]{2,1,0:T(8,128)(2,1)}), bf16[16,144,128]{2,1,0:T(8,128)(2,1)S(1)}, u32[]{:S(2)}, u32[]{:S(2)}) %all-to-all-start) | async-done | bytes 589856 | tf_op jit(solution)/shard_map/all_to_all | solution.py:288
  35.5 0.0 copy-start
  35.5 0.9 copy-done
  36.4 2.2 %shard_map.120 = bf16[16,128,128]{2,1,0:T(8,128)(2,1)} custom-call(bf16[16,144,128]{2,1,0:T(8,128)(2,1)} %copy-done, bf16[16,144,128]{2,1,0:T(8,128)(2,1)} %copy-done, bf16[512,2048]{1,0:T(8,128)(2,1)} %get-tuple-element.32.ordered_ref.inner_ref), custom_call_target="tpu_custom_call" | custom-call | tf_op jit(solution)/shard_map/pallas_call | solution.py:281
  38.6 14.9 %all_to_all.29.in_ref = bf16[16,128,128]{2,1,0:T(8,128)(2,1)} all-to-all(bf16[16,128,128]{2,1,0:T(8,128)(2,1)} %shard_map.120), channel_id=1, replica_groups=mesh['y'=4,'core'=2,'z'=4,'x'=4] {'z','x'}, dimensions={0} | all-to-all | bytes 1048576 | tf_op jit(solution)/shard_map/all_to_all | solution.py:296
  53.5 12.8 %shard_map.121 = (bf16[512,2048]{1,0:T(8,128)(2,1)}, f32[16,2048]{1,0:T(8,128)}, f32[4,512,4]{2,1,0:T(8,128)}, bf16[512,2048]{1,0:T(8,128)(2,1)}, bf16[2048,2048]{1,0:T(8,128)(2,1)}) custom-call(bf16[512,2048]{1,0:T(8,128)(2,1)} %get-tuple-element.32.ordered_ref.inner_ref, f32[16,2048]{1,0:T(8,128)} %get-tuple-element.33.top_ref, ...), custom_call_target="tpu_custom_call" | custom-call | flops 7200000000 | bytes 30000000 | tf_op jit(solution)/shard_map/pallas_call | solution.py:298
  66.3 0.0 reduce-scatter.2.cloned.1.call-update
  66.3 0.0 all-gather.2.cloned.1.call-done.weight_ref
  66.3 14.5 %shard_map.122 = (bf16[512,2048]{1,0:T(8,128)(2,1)}, bf16[512,2048]{1,0:T(8,128)(2,1)}, bf16[16,2048]{1,0:T(8,128)(2,1)}, bf16[16,128,128]{2,1,0:T(8,128)(2,1)}, bf16[16,128,128]{2,1,0:T(8,128)(2,1)}) custom-call(bf16[512,2048]{1,0:T(8,128)(2,1)} %bitcast.16, bf16[2048,2048]{1,0:T(8,128)(2,1)} %all-gather.2.cloned.1.call-done.weight_ref, ...), custom_call_target="tpu_custom_call" | custom-call | flops 7200000000 | bytes 30000000 | tf_op jit(solution)/shard_map/pallas_call | solution.py:314
  80.8 3.6 %all-to-all-start.2 = ((bf16[16,128,128]{2,1,0:T(8,128)(2,1)}), bf16[16,128,128]{2,1,0:T(8,128)(2,1)S(1)}, u32[]{:S(2)}, u32[]{:S(2)}) async-start(bf16[16,128,128]{2,1,0:T(8,128)(2,1)} %get-tuple-element.42.ordered_ref), calls=%async_computation.2 | async-start | bytes 1048576 | tf_op jit(solution)/shard_map/all_to_all | solution.py:330
  84.4 8.9 %shard_map.123.ordered_ref = bf16[512,2048]{1,0:T(8,128)(2,1)} custom-call(bf16[512,2048]{1,0:T(8,128)(2,1)} %get-tuple-element.38.hidden_ref, bf16[2048,2048]{1,0:T(8,128)(2,1)} %all-gather.2.cloned.1.call-done.weight_ref, bf16[16,128,128]{2,1,0:T(8,128)(2,1)} %get-tuple-element.42.ordered_ref), custom_call_target="tpu_custom_call" | custom-call | flops 4800000000 | bytes 20000000 | tf_op jit(solution)/shard_map/pallas_call | solution.py:331
  93.3 1.5 %all-to-all-done.2.parts_ref = bf16[16,128,128]{2,1,0:T(8,128)(2,1)S(1)} async-done(((bf16[16,128,128]{2,1,0:T(8,128)(2,1)}), bf16[16,128,128]{2,1,0:T(8,128)(2,1)S(1)}, u32[]{:S(2)}, u32[]{:S(2)}) %all-to-all-start.2) | async-done | bytes 524320 | tf_op jit(solution)/shard_map/all_to_all | solution.py:330
  94.8 0.0 copy-start.1
  94.8 0.8 copy-done.1
  95.6 2.2 %shard_map.124.ordered_ref = bf16[16,128,128]{2,1,0:T(8,128)(2,1)} custom-call(bf16[16,128,128]{2,1,0:T(8,128)(2,1)} %copy-done.1, bf16[16,144,128]{2,1,0:T(8,128)(2,1)} %copy-done, bf16[512,2048]{1,0:T(8,128)(2,1)} %shard_map.123.ordered_ref), custom_call_target="tpu_custom_call" | custom-call | tf_op jit(solution)/shard_map/pallas_call | solution.py:281
  97.8 5.7 %all-to-all-start.3 = ((bf16[16,128,128]{2,1,0:T(8,128)(2,1)}), bf16[16,128,128]{2,1,0:T(8,128)(2,1)S(1)}, u32[]{:S(2)}, u32[]{:S(2)}) async-start(bf16[16,128,128]{2,1,0:T(8,128)(2,1)} %shard_map.124.ordered_ref), calls=%async_computation.3 | async-start | bytes 1048576 | tf_op jit(solution)/shard_map/all_to_all | solution.py:343
  103.4 14.2 %shard_map.125 = (bf16[512,2048]{1,0:T(8,128)(2,1)}, bf16[512,2048]{1,0:T(8,128)(2,1)}, bf16[512,2048]{1,0:T(8,128)(2,1)}) custom-call(bf16[512,2048]{1,0:T(8,128)(2,1)} %bitcast.19, bf16[512,2048]{1,0:T(8,128)(2,1)} %bitcast.22, bf16[512,2048]{1,0:T(8,128)(2,1)} %bitcast.26, bf16[512,2048]{1,0:T(8,128)(2,1)} %get-tuple-element.43.dm_ref, ...), custom_call_target="tpu_custom_call" | custom-call | flops 7800000000 | bytes 32500000 | tf_op jit(solution)/shard_map/pallas_call | solution.py:344
  117.6 0.0 reduce-scatter.2.cloned.1.call-done
  117.6 0.0 all-to-all-done.3.ret_ref
  117.7 0.0 copy-start.2
  117.7 7.2 %all-to-all-start.4 = ((bf16[16,16,2048]{2,1,0:T(8,128)(2,1)}), bf16[16,16,2048]{2,1,0:T(8,128)(2,1)S(1)}, u32[]{:S(2)}, u32[]{:S(2)}) async-start(bf16[16,16,2048]{2,1,0:T(8,128)(2,1)} %bitcast.12), calls=%async_computation.5 | async-start | bytes 2097152 | tf_op jit(solution)/shard_map/all_to_all | solution.py:357
  124.9 0.0 copy-done.2
  124.9 7.2 %shard_map.126 = (bf16[512,2048]{1,0:T(8,128)(2,1)}, bf16[512,2048]{1,0:T(8,128)(2,1)}) custom-call(bf16[512,2048]{1,0:T(8,128)(2,1)} %bitcast.23, bf16[512,2048]{1,0:T(8,128)(2,1)} %bitcast.27, bf16[512,2048]{1,0:T(8,128)(2,1)} %get-tuple-element.46.pk_ref, bf16[512,2048]{1,0:T(8,128)(2,1)} %get-tuple-element.47.pv_ref, ...), custom_call_target="tpu_custom_call" | custom-call | flops 3000000000 | bytes 12500000 | tf_op jit(solution)/shard_map/pallas_call | solution.py:351
  132.1 8.8 %all-to-all-done.4 = bf16[16,16,2048]{2,1,0:T(8,128)(2,1)S(1)} async-done(((bf16[16,16,2048]{2,1,0:T(8,128)(2,1)}), bf16[16,16,2048]{2,1,0:T(8,128)(2,1)S(1)}, u32[]{:S(2)}, u32[]{:S(2)}) %all-to-all-start.4) | async-done | bytes 1048608 | tf_op jit(solution)/shard_map/all_to_all | solution.py:357
  140.9 0.1 convert_reduce_fusion
  141.1 0.7 broadcast_multiply_fusion
Async XLA Ops:
  7.2 59.2 %all-gather.2.cloned.1.call-start = ((), (), s32[]{:S(2)}) async-start(), calls=%async_computation.6 | async-start | bytes 9437184 | tf_op jit(solution)/shard_map/all_gather | solution.py:272
  15.3 20.2 %all-to-all-start = ((bf16[16,144,128]{2,1,0:T(8,128)(2,1)}), bf16[16,144,128]{2,1,0:T(8,128)(2,1)S(1)}, u32[]{:S(2)}, u32[]{:S(2)}) async-start(bf16[16,144,128]{2,1,0:T(8,128)(2,1)} %get-tuple-element.36), calls=%async_computation | async-start | bytes 1179648 | tf_op jit(solution)/shard_map/all_to_all | solution.py:288
  23.3 94.3 %reduce-scatter.2.cloned.1.call-start = ((), (), s32[]{:S(2)}) async-start(), calls=%async_computation.7 | async-start | bytes 9437184 | tf_op jit(solution)/shard_map/reduce_scatter | solution.py:312
  35.5 0.9 copy-start
  80.8 14.0 %all-to-all-start.2 = ((bf16[16,128,128]{2,1,0:T(8,128)(2,1)}), bf16[16,128,128]{2,1,0:T(8,128)(2,1)S(1)}, u32[]{:S(2)}, u32[]{:S(2)}) async-start(bf16[16,128,128]{2,1,0:T(8,128)(2,1)} %get-tuple-element.42.ordered_ref), calls=%async_computation.2 | async-start | bytes 1048576 | tf_op jit(solution)/shard_map/all_to_all | solution.py:330
  94.8 0.8 copy-start.1
  97.8 19.9 %all-to-all-start.3 = ((bf16[16,128,128]{2,1,0:T(8,128)(2,1)}), bf16[16,128,128]{2,1,0:T(8,128)(2,1)S(1)}, u32[]{:S(2)}, u32[]{:S(2)}) async-start(bf16[16,128,128]{2,1,0:T(8,128)(2,1)} %shard_map.124.ordered_ref), calls=%async_computation.3 | async-start | bytes 1048576 | tf_op jit(solution)/shard_map/all_to_all | solution.py:343
  117.7 7.2 %copy-start.2 = (bf16[16,128,128]{2,1,0:T(8,128)(2,1)}, bf16[16,128,128]{2,1,0:T(8,128)(2,1)S(1)}, u32[]{:S(2)}) copy-start(bf16[16,128,128]{2,1,0:T(8,128)(2,1)S(1)} %all-to-all-done.3.ret_ref) | copy-start | bytes 1572868
  117.7 23.3 %all-to-all-start.4 = ((bf16[16,16,2048]{2,1,0:T(8,128)(2,1)}), bf16[16,16,2048]{2,1,0:T(8,128)(2,1)S(1)}, u32[]{:S(2)}, u32[]{:S(2)}) async-start(bf16[16,16,2048]{2,1,0:T(8,128)(2,1)} %bitcast.12), calls=%async_computation.5 | async-start | bytes 2097152 | tf_op jit(solution)/shard_map/all_to_all | solution.py:357
Sparse Core Ops, SparseCore 0:
  9.7 52.1 all-gather.1
  66.4 50.5 reduce-scatter.1
